TPU v7x, 32 devices: a whole 2x2x4 slice. The times are simulated.
32 devices in a mesh: parts: 2 (over x), loop: 2 (over core), width: 8 (over z, y).
Axes of the slice: x: 2, y: 2, z: 4, core: 2. Of those that a mesh axis runs over, the one named last changes fastest.
Arguments:
- queries: float32 [2048, 65536], P(('parts', 'loop'), 'width'), parts along dimension 0, may hold values from -6 to 6
- store: float32 [4096, 65536], P(('parts', 'loop'), 'width'), parts along dimension 0, may hold values from -0.03125 to 0.03125
Outputs:
- scores: float32 [4096, 1024], P(('parts', 'loop', 'width')), parts along dimension 0
There are 2 independent parts, one for each index of `parts`. A program takes and returns all parts, laid end to end along the dimension named above; each array names one. Nothing has to cross between parts.
All inputs are finite; a program needn't handle non-finite values.
Results may differ from a plain program's by a relative error of at most 0.000071.
Values sent between devices are 32-bit elements; how exact they have to be, the bound alone decides.
A program may use at most 192 MiB of HBM per device.

v0:
```python
import jax
import jax.numpy as jnp
from jax import lax
from jax.sharding import PartitionSpec as P


def shifted(value, axis, steps):
    count = lax.axis_size(axis)
    pairs = [(source, (source + steps) % count) for source in range(count)]
    return lax.ppermute(value, axis, pairs)


def partial_scores(store, panel):
    return lax.dot_general(
        store,
        panel,
        (((1,), (1,)), ((), ())),
        precision=lax.Precision.HIGHEST,
        preferred_element_type=jnp.float32,
    )


def body(queries, store):
    panel_rows = queries.shape[0]
    store_rows = store.shape[0]
    loop_size = lax.axis_size("loop")
    here = lax.axis_index("loop")
    panel = queries
    collected = jnp.zeros((store_rows, panel_rows * loop_size), jnp.float32)
    for step in range(loop_size):
        owner = (here - step) % loop_size
        local_part = partial_scores(store, panel)
        collected = lax.dynamic_update_slice_in_dim(collected, local_part, owner * panel_rows, 1)
        if step + 1 < loop_size:
            panel = shifted(panel, "loop", 1)
    collected = lax.psum_scatter(collected, "width", scatter_dimension=0, tiled=True)
    return collected


def solution(mesh):
    in_specs = (P(("parts", "loop"), "width"), P(("parts", "loop"), "width"))
    out_specs = P(("parts", "loop", "width"), None)
    return jax.shard_map(body, mesh=mesh, in_specs=in_specs, out_specs=out_specs, check_vma=False)
```

profile of v0, /device:TPU:0, one launch (start us, length us, event | category | flops | bytes accessed | tf_op | source)
XLA Modules:
  0.0 226.8 jit_solution(2692346624066217495)
XLA Ops:
  6.5 0.0 reduce-scatter.2.cloned.1.call-start
  6.5 0.5 collective-permute-start
  7.0 2.5 %broadcast_in_dim.3 = f32[1024,1024]{1,0:T(8,128)} broadcast(f32[]{:T(128)} %constant.24.clone.1), dimensions={} | broadcast | bytes 4194308 | tf_op jit(solution)/shard_map/broadcast_in_dim | solution.py:29
  9.4 59.7 %convolution_dynamic-update-slice_fusion.1 = f32[1024,1024]{1,0:T(8,128)} fusion(f32[1024,1024]{1,0:T(8,128)} %broadcast_in_dim.3, s32[]{:T(128)S(6)} %select_n.18, f32[1024,8192]{1,0:T(8,128)} %param.3, f32[512,8192]{1,0:T(8,128)} %param.2), kind=kOutput, calls=%fused_computation.1 | convolution fusion | flops 51539607552 | bytes 52428804 | tf_op jit(solution)/shard_map/dot_general | solution.py:14
  69.2 0.0 collective-permute-done
  69.2 59.7 %convolution_dynamic-update-slice_fusion = f32[1024,1024]{1,0:T(8,128)} fusion(f32[1024,1024]{1,0:T(8,128)} %convolution_dynamic-update-slice_fusion.1, s32[]{:T(128)S(6)} %select_n.20, f32[1024,8192]{1,0:T(8,128)} %param.3, f32[512,8192]{1,0:T(8,128)} %collective-permute-done), kind=kOutput, calls=%fused_computation | convolution fusion | flops 51539607552 | bytes 52428804 | tf_op jit(solution)/shard_map/dot_general | solution.py:14
  128.9 0.0 reduce-scatter.2.cloned.1.call-update
  129.0 91.0 %reduce-scatter.2.cloned.1.call-done = f32[128,1024]{1,0:T(8,128)} async-done(((f32[1024,1024]{1,0:T(8,128)}), f32[128,1024]{1,0:T(8,128)}) %reduce-scatter.2.cloned.1.call-update) | async-done | bytes 524304 | tf_op jit(solution)/shard_map/reduce_scatter | solution.py:36
Async XLA Ops:
  6.5 213.4 %reduce-scatter.2.cloned.1.call-start = ((), (), s32[]{:S(2)}) async-start(), calls=%async_computation.1 | async-start | bytes 4718592 | tf_op jit(solution)/shard_map/reduce_scatter | solution.py:36
  6.5 62.7 %collective-permute-start = (f32[512,8192]{1,0:T(8,128)}, f32[512,8192]{1,0:T(8,128)}, u32[]{:S(2)}, u32[]{:S(2)}) collective-permute-start(f32[512,8192]{1,0:T(8,128)} %param.2), channel_id=1, source_target_pairs={{0,8},{8,0},{1,9},{9,1},{2,10},{10,2},{3,11},{11,3},{4,12},{12,4},... | collective-permute-start | bytes 50331656 | tf_op jit(solution)/shard_map/ppermute | solution.py:10
Sparse Core Ops, SparseCore 0:
  129.1 90.8 reduce-scatter.1
where the time goes:
time: 227 us
  matrix products  119 us (52%)
  waiting for transfers between devices  91 us (40%)
  between operations  13.4 us (6%)
  local copies, waits for them, and re-layouts  2.46 us (1%)
    dot_general x2, matrix products, partial_scores(): lax.dot_general(store, panel, (((1,), (1,)), ((), ())), precision=lax.Pre...  119 us
    reduce_scatter x1, waiting for transfers between devices, body(): lax.psum_scatter(collected, 'width', scatter_dimension=0, tiled=True)  91 us
  transfers between devices with their start and end apart: 2, of which 1 were waited for; matrix products, arithmetic and copies ran while one was open for 27% of the time, Pallas kernels for 0%

commit v1 on v0

--- a/solution.py
+++ b/solution.py
@@ -15,26 +15,26 @@
         store,
         panel,
         (((1,), (1,)), ((), ())),
-        precision=lax.Precision.HIGHEST,
+        precision=lax.Precision.HIGH,
         preferred_element_type=jnp.float32,
     )
 
 
 def body(queries, store):
     panel_rows = queries.shape[0]
-    store_rows = store.shape[0]
     loop_size = lax.axis_size("loop")
     here = lax.axis_index("loop")
     panel = queries
-    collected = jnp.zeros((store_rows, panel_rows * loop_size), jnp.float32)
+    rows = store.shape[0] // lax.axis_size("width")
+    out = jnp.zeros((rows, panel_rows * loop_size), jnp.float32)
     for step in range(loop_size):
         owner = (here - step) % loop_size
-        local_part = partial_scores(store, panel)
-        collected = lax.dynamic_update_slice_in_dim(collected, local_part, owner * panel_rows, 1)
+        part = partial_scores(store, panel)
         if step + 1 < loop_size:
             panel = shifted(panel, "loop", 1)
-    collected = lax.psum_scatter(collected, "width", scatter_dimension=0, tiled=True)
-    return collected
+        part = lax.psum_scatter(part, "width", scatter_dimension=0, tiled=True)
+        out = lax.dynamic_update_slice_in_dim(out, part, owner * panel_rows, 1)
+    return out
 
 
 def solution(mesh):

time: 227 us -> 189 us (0.83)
  matrix products: 119 us -> 65.7 us
  waiting for transfers between devices: 91 us -> 107 us
    dot_general x2, matrix products: 119 us -> 65.7 us  [partial_scores(): lax.dot_general(store, panel, (((1,), (1,)), ((), ())), precision=lax.Pre...]
    reduce_scatter x1 -> x2, waiting for transfers between devices: 91 us -> 107 us  [body(): part = lax.psum_scatter(part, 'width', scatter_dimension=0, tiled=True)]
    dynamic_update_slice x0 -> x2, local copies, waits for them, and re-layouts: none -> 2.65 us  [body(): out = lax.dynamic_update_slice_in_dim(out, part, owner * panel_rows, 1)]
    broadcast_in_dim x1, local copies, waits for them, and re-layouts: 2.46 us -> 0.04 us  [body(): out = jnp.zeros((rows, panel_rows * loop_size), jnp.float32)]
  transfers between devices with their start and end apart: 2 -> 3, of which waited for: 1 -> 2; matrix products, arithmetic and copies ran while one was open for 27% -> 35% of each run, Pallas kernels for 0% -> 0%
where the time goes in v1:
time: 189 us
  waiting for transfers between devices  107 us (57%)
  matrix products  65.7 us (35%)
  between operations  13.5 us (7%)
  local copies, waits for them, and re-layouts  2.69 us (1%)
    reduce_scatter x2, waiting for transfers between devices, body(): part = lax.psum_scatter(part, 'width', scatter_dimension=0, tiled=True)  107 us
    dot_general x2, matrix products, partial_scores(): lax.dot_general(store, panel, (((1,), (1,)), ((), ())), precision=lax.Pre...  65.7 us
  transfers between devices with their start and end apart: 3, of which 2 were waited for; matrix products, arithmetic and copies ran while one was open for 35% of the time, Pallas kernels for 0%

profile of v1, /device:TPU:0, one launch (start us, length us, event | category | flops | bytes accessed | tf_op | source)
XLA Modules:
  0.0 189.2 jit_solution(11559819259423566641)
XLA Ops:
  6.5 0.0 reduce-scatter.3.cloned.1.call-start
  6.5 0.5 collective-permute-start
  7.0 32.9 %fusion = f32[1024,512]{1,0:T(8,128)} fusion(f32[1024,8192]{1,0:T(8,128)} %param.3, f32[512,8192]{1,0:T(8,128)} %param.2), kind=kOutput, calls=%fused_computation.2 | convolution fusion | flops 25769803776 | bytes 52428800 | tf_op jit(solution)/shard_map/dot_general | solution.py:14
  39.8 0.0 reduce-scatter.3.cloned.1.call-update
  39.9 0.2 reduce-scatter.5.cloned.1.call-start
  40.1 0.0 collective-permute-done
  40.1 32.8 %fusion.1 = f32[1024,512]{1,0:T(8,128)} fusion(f32[1024,8192]{1,0:T(8,128)} %param.3, f32[512,8192]{1,0:T(8,128)} %collective-permute-done), kind=kOutput, calls=%fused_computation.3 | convolution fusion | flops 25769803776 | bytes 52428800 | tf_op jit(solution)/shard_map/dot_general | solution.py:14
  72.9 0.0 reduce-scatter.5.cloned.1.call-update
  73.0 37.2 %reduce-scatter.3.cloned.1.call-done = f32[128,512]{1,0:T(8,128)} async-done(((f32[1024,512]{1,0:T(8,128)}), f32[128,512]{1,0:T(8,128)}) %reduce-scatter.3.cloned.1.call-update) | async-done | bytes 262160 | tf_op jit(solution)/shard_map/reduce_scatter | solution.py:35
  110.3 1.0 constant_dynamic-update-slice_fusion.1
  111.2 0.0 copy-start
  111.3 69.4 %reduce-scatter.5.cloned.1.call-done = f32[128,512]{1,0:T(8,128)} async-done(((f32[1024,512]{1,0:T(8,128)}), f32[128,512]{1,0:T(8,128)}) %reduce-scatter.5.cloned.1.call-update) | async-done | bytes 262160 | tf_op jit(solution)/shard_map/reduce_scatter | solution.py:35
  180.7 0.0 copy-done
  180.7 1.7 constant_dynamic-update-slice_fusion
  (1 shorter events, 0.0 us)
Async XLA Ops:
  6.5 103.7 %reduce-scatter.3.cloned.1.call-start = ((), (), s32[]{:S(2)}) async-start(), calls=%async_computation.2 | async-start | bytes 2359296 | tf_op jit(solution)/shard_map/reduce_scatter | solution.py:35
  6.5 33.6 %collective-permute-start = (f32[512,8192]{1,0:T(8,128)}, f32[512,8192]{1,0:T(8,128)}, u32[]{:S(2)}, u32[]{:S(2)}) collective-permute-start(f32[512,8192]{1,0:T(8,128)} %param.2), channel_id=1, source_target_pairs={{0,8},{8,0},{1,9},{9,1},{2,10},{10,2},{3,11},{11,3},{4,12},{12,4},... | collective-permute-start | bytes 50331656 | tf_op jit(solution)/shard_map/ppermute | solution.py:10
  39.9 140.8 %reduce-scatter.5.cloned.1.call-start = ((), (), s32[]{:S(2)}) async-start(), calls=%async_computation.3 | async-start | bytes 2359296 | tf_op jit(solution)/shard_map/reduce_scatter | solution.py:35
  111.2 69.4 %copy-start = (f32[128,1024]{1,0:T(8,128)}, f32[128,1024]{1,0:T(8,128)S(1)}, u32[]{:S(2)}) copy-start(f32[128,1024]{1,0:T(8,128)S(1)} %constant_dynamic-update-slice_fusion.1) | copy-start | bytes 1572868
Sparse Core Ops, SparseCore 0:
  40.0 70.1 reduce-scatter.2
  113.7 66.8 reduce-scatter.4

commit v2 on v1

v2 whole, which is shorter than its diff:
```python
import functools

import jax
import jax.numpy as jnp
from jax import lax
from jax.experimental import pallas as pl
from jax.experimental.pallas import tpu as pltpu
from jax.sharding import PartitionSpec as P

MESH = pl.DeviceIdType.MESH
PIECES = 4


def split(value):
    high = value.astype(jnp.bfloat16)
    low = (value - high.astype(jnp.float32)).astype(jnp.bfloat16)
    return high, low


def dot_t(left, right):
    return lax.dot_general(
        left, right, (((1,), (1,)), ((), ())), preferred_element_type=jnp.float32
    )


def kernel(width, group_rows, cols, depth, q_ref, s_ref, out_ref, rq_ref,
           s_hi, s_lo, q_hi, q_lo, s_stage, q_stage, res, rx1, rx2,
           s_sem, q_sem, xs_sem, xr_sem, as_sem, ar_sem, bs_sem, br_sem):
    here = lax.axis_index("loop")
    me = lax.axis_index("width")
    line, side = me // 2, me % 2
    pairs = width // 2
    store_rows, extent = s_ref.shape
    own = store_rows // width
    groups = store_rows // group_rows
    per_group = pairs // groups
    steps = extent // depth
    panel_rows = q_ref.shape[0]
    own_chunks = panel_rows // cols
    chunks = 2 * own_chunks
    piece = cols // PIECES
    order = []
    for i in range((pairs + 1) // 2):
        order += [i] if i == pairs - 1 - i else [i, pairs - 1 - i]

    barrier = pltpu.get_barrier_semaphore()
    pl.semaphore_signal(barrier, inc=1, device_id={"loop": 1 - here}, device_id_type=MESH)
    pl.semaphore_signal(barrier, inc=1, device_id={"width": line * 2 + 1 - side}, device_id_type=MESH)
    for other in range(1, pairs):
        target = lax.rem(line + other, pairs) * 2 + side
        pl.semaphore_signal(barrier, inc=1, device_id={"width": target}, device_id_type=MESH)

    def s_copies(g, kb, slot):
        return [
            pltpu.make_async_copy(
                s_ref.at[pl.ds(order[g * per_group + k] * 2 * own, 2 * own), pl.ds(pl.multiple_of(kb * depth, depth), depth)],
                s_stage.at[slot, pl.ds(k * 2 * own, 2 * own)],
                s_sem.at[slot, k],
            )
            for k in range(per_group)
        ]

    def q_copy(c, kb, slot):
        source, first = (q_ref, c) if c < own_chunks else (rq_ref, c - own_chunks)
        return pltpu.make_async_copy(
            source.at[pl.ds(first * cols, cols), pl.ds(pl.multiple_of(kb * depth, depth), depth)],
            q_stage.at[slot],
            q_sem.at[slot],
        )

    def exchange(c, m):
        rows = pl.ds(c * cols + m * piece, piece)
        return pltpu.make_async_remote_copy(
            src_ref=q_ref.at[rows], dst_ref=rq_ref.at[rows],
            send_sem=xs_sem.at[c, m], recv_sem=xr_sem.at[c, m],
            device_id={"loop": 1 - here}, device_id_type=MESH,
        )

    def stage_a(u):
        return pltpu.make_async_remote_copy(
            src_ref=res.at[u, :, 1 - side], dst_ref=rx1.at[u],
            send_sem=as_sem.at[u], recv_sem=ar_sem.at[u],
            device_id={"width": line * 2 + 1 - side}, device_id_type=MESH,
        )

    def stage_b(u, k):
        c, g = u // groups, u % groups
        p = order[g * per_group + k]
        return pltpu.make_async_remote_copy(
            src_ref=res.at[u, k, side], dst_ref=rx2.at[line, c],
            send_sem=bs_sem.at[u, k], recv_sem=br_sem.at[line, c],
            device_id={"width": p * 2 + side}, device_id_type=MESH,
        )

    def receive_b(c, source):
        return pltpu.make_async_remote_copy(
            src_ref=rx2.at[source, c], dst_ref=rx2.at[source, c],
            send_sem=bs_sem.at[0, 0], recv_sem=br_sem.at[source, c],
            device_id={"width": source * 2 + side}, device_id_type=MESH,
        )

    def pass_on(u):
        c, g = u // groups, u % groups
        stage_a(u).wait_recv()
        for k in range(per_group):
            res[u, k, side] = res[u, k, side] + rx1[u, k]
            p = order[g * per_group + k]

            @pl.when(p != line)
            def _():
                stage_b(u, k).start()

            @pl.when(p == line)
            def _():
                rx2[line, c] = res[u, k, side]

    def finish(c):
        for source in range(pairs):
            @pl.when(source != line)
            def _():
                receive_b(c, source).wait_recv()
        total = rx2[0, c]
        for source in range(1, pairs):
            total = total + rx2[source, c]
        owner = here if c < own_chunks else 1 - here
        start = pl.multiple_of(owner * panel_rows + (c % own_chunks) * cols, cols)
        out_ref[:, pl.ds(start, cols)] = total

    for copy in s_copies(0, 0, 0):
        copy.start()
    q_copy(0, 0, 0).start()
    pl.semaphore_wait(barrier, pairs + 1)
    for c in range(own_chunks):
        for m in range(PIECES):
            exchange(c, m).start()

    units = chunks * groups
    for u in range(units):
        c, g = u // groups, u % groups
        refill = g == groups - 1 and c + 1 < chunks
        res[u] = jnp.zeros(res.shape[1:], jnp.float32)
        if refill:
            if c + 1 >= own_chunks:
                for m in range(PIECES):
                    exchange(c + 1 - own_chunks, m).wait_recv()
            q_copy(c + 1, 0, 0).start()

        @pl.loop(0, steps)
        def _(kb):
            slot = lax.rem(kb, 2)
            if c == 0:
                @pl.when(kb + 1 < steps)
                def _():
                    for copy in s_copies(g, kb + 1, 1 - slot):
                        copy.start()
            if u == 0 or refill:
                @pl.when(kb + 1 < steps)
                def _():
                    q_copy(0 if u == 0 else c + 1, kb + 1, 1 - slot).start()
            if c == 0:
                for copy in s_copies(g, kb, slot):
                    copy.wait()
                s_hi[g, kb], s_lo[g, kb] = split(s_stage[slot])
            if u == 0:
                q_copy(0, kb, slot).wait()
                q_hi[kb], q_lo[kb] = split(q_stage[slot])
            high = s_hi[g, kb]
            part = dot_t(high, q_hi[kb]) + dot_t(s_lo[g, kb], q_hi[kb]) + dot_t(high, q_lo[kb])
            res[u] += part.reshape(res.shape[1:])
            if refill:
                q_copy(c + 1, kb, slot).wait()
                q_hi[kb], q_lo[kb] = split(q_stage[slot])

        stage_a(u).start()
        if c == 0 and g + 1 < groups:
            for copy in s_copies(g + 1, 0, 0):
                copy.start()
        if u >= 1:
            pass_on(u - 1)
    for c in range(chunks - 1):
        finish(c)
    pass_on(units - 1)
    finish(chunks - 1)
    for u in range(units):
        stage_a(u).wait_send()
        for k in range(per_group):
            @pl.when(order[u % groups * per_group + k] != line)
            def _():
                stage_b(u, k).wait_send()
    for c in range(own_chunks):
        for m in range(PIECES):
            exchange(c, m).wait_send()


def body(width, queries, store):
    panel_rows, extent = queries.shape
    store_rows = store.shape[0]
    own = store_rows // width
    group_rows, cols, depth = 512, 256, 1024
    groups, steps = store_rows // group_rows, extent // depth
    chunks = 2 * panel_rows // cols
    pairs = width // 2
    per_group = pairs // groups
    units = chunks * groups
    f32, bf16 = jnp.float32, jnp.bfloat16
    dma = pltpu.SemaphoreType.DMA
    out, _ = pl.pallas_call(
        functools.partial(kernel, width, group_rows, cols, depth),
        out_shape=(
            jax.ShapeDtypeStruct((own, 2 * panel_rows), f32),
            jax.ShapeDtypeStruct((panel_rows, extent), f32),
        ),
        in_specs=[pl.BlockSpec(memory_space=pl.ANY)] * 2,
        out_specs=(pl.BlockSpec(memory_space=pltpu.VMEM), pl.BlockSpec(memory_space=pl.ANY)),
        scratch_shapes=[
            pltpu.VMEM((groups, steps, group_rows, depth), bf16),
            pltpu.VMEM((groups, steps, group_rows, depth), bf16),
            pltpu.VMEM((steps, cols, depth), bf16),
            pltpu.VMEM((steps, cols, depth), bf16),
            pltpu.VMEM((2, group_rows, depth), f32),
            pltpu.VMEM((2, cols, depth), f32),
            pltpu.VMEM((units, per_group, 2, own, cols), f32),
            pltpu.VMEM((units, per_group, own, cols), f32),
            pltpu.VMEM((pairs, chunks, own, cols), f32),
            dma((2, per_group)),
            dma((2,)),
            dma((chunks // 2, PIECES)),
            dma((chunks // 2, PIECES)),
            dma((units,)),
            dma((units,)),
            dma((units, per_group)),
            dma((pairs, chunks)),
        ],
        compiler_params=pltpu.CompilerParams(
            collective_id=0, has_side_effects=True, vmem_limit_bytes=62 * 2**20
        ),
        cost_estimate=pl.CostEstimate(
            flops=12 * store_rows * panel_rows * extent,
            bytes_accessed=4 * extent * (store_rows + 3 * panel_rows),
            transcendentals=0,
        ),
    )(queries, store)
    return out


def solution(mesh):
    in_specs = (P(("parts", "loop"), "width"), P(("parts", "loop"), "width"))
    out_specs = P(("parts", "loop", "width"), None)
    step = functools.partial(body, mesh.shape["width"])
    return jax.shard_map(step, mesh=mesh, in_specs=in_specs, out_specs=out_specs, check_vma=False)
```

time: 189 us -> 97.7 us (0.52)
  waiting for transfers between devices: 107 us -> 0 us
  Pallas kernels: 0 us -> 95.6 us
  matrix products: 65.7 us -> 0 us
  between operations: 13.5 us -> 0.01 us
    reduce_scatter x2 -> x0, waiting for transfers between devices: 107 us -> none  [body(): part = lax.psum_scatter(part, 'width', scatter_dimension=0, tiled=True)]
    pallas_call x0 -> x1, Pallas kernels: none -> 95.6 us  [body(): pl.pallas_call(functools.partial(kernel, width, group_rows, cols, depth),...]
    dot_general x2 -> x0, matrix products: 65.7 us -> none  [partial_scores(): lax.dot_general(store, panel, (((1,), (1,)), ((), ())), precision=lax.Pre...]
    dynamic_update_slice x2 -> x0, local copies, waits for them, and re-layouts: 2.65 us -> none  [body(): out = lax.dynamic_update_slice_in_dim(out, part, owner * panel_rows, 1)]
  transfers between devices with their start and end apart: 3 -> 0, of which waited for: 2 -> 0; matrix products, arithmetic and copies ran while one was open for 35% -> 0% of each run, Pallas kernels for 0% -> 0%
where the time goes in v2:
time: 97.7 us; the launch traced here: 97.5 us
  Pallas kernels  95.6 us (98%)
  local copies, waits for them, and re-layouts  1.89 us (2%)
    pallas_call x1, Pallas kernels, body(): pl.pallas_call(functools.partial(kernel, width, group_rows, cols, depth),...  95.6 us

profile of v2, /device:TPU:0, one launch (start us, length us, event | category | flops | bytes accessed | tf_op | source)
XLA Modules:
  0.0 97.5 jit_solution(14341089510084947134)
XLA Ops:
  0.0 95.6 %shard_map.28 = (f32[128,1024]{1,0:T(8,128)}, f32[512,8192]{1,0:T(8,128)}) custom-call(f32[512,8192]{1,0:T(8,128)} %q_ref.1, f32[1024,8192]{1,0:T(8,128)} %s_ref.1), custom_call_target="tpu_custom_call" | custom-call | flops 51539607552 | bytes 83886080 | tf_op jit(solution)/shard_map/pallas_call | solution.py:207
  95.6 1.9 %copy.4 = f32[128,1024]{1,0:T(8,128)} copy(f32[128,1024]{1,0:T(8,128)} %get-tuple-element.6) | data formatting | bytes 1048576

commit v3 on v2

--- a/solution.py
+++ b/solution.py
@@ -165,7 +165,10 @@
                 q_copy(0, kb, slot).wait()
                 q_hi[kb], q_lo[kb] = split(q_stage[slot])
             high = s_hi[g, kb]
-            part = dot_t(high, q_hi[kb]) + dot_t(s_lo[g, kb], q_hi[kb]) + dot_t(high, q_lo[kb])
+            part = dot_t(
+                jnp.concatenate([high, s_lo[g, kb], high], 1),
+                jnp.concatenate([q_hi[kb], q_hi[kb], q_lo[kb]], 1),
+            )
             res[u] += part.reshape(res.shape[1:])
             if refill:
                 q_copy(c + 1, kb, slot).wait()

time: 97.7 us -> 98 us (level)
  no operation moved by 1% of the time
where the time goes in v3:
time: 98 us; the launch traced here: 97.6 us
  Pallas kernels  95.7 us (98%)
  local copies, waits for them, and re-layouts  1.89 us (2%)
    pallas_call x1, Pallas kernels, body(): pl.pallas_call(functools.partial(kernel, width, group_rows, cols, depth),...  95.7 us

profile of v3, /device:TPU:0, one launch (start us, length us, event | category | flops | bytes accessed | tf_op | source)
XLA Modules:
  0.0 97.6 jit_solution(15823366604627919101)
XLA Ops:
  0.0 95.7 %shard_map.28 = (f32[128,1024]{1,0:T(8,128)}, f32[512,8192]{1,0:T(8,128)}) custom-call(f32[512,8192]{1,0:T(8,128)} %q_ref.1, f32[1024,8192]{1,0:T(8,128)} %s_ref.1), custom_call_target="tpu_custom_call" | custom-call | flops 51539607552 | bytes 83886080 | tf_op jit(solution)/shard_map/pallas_call | solution.py:210
  95.7 1.9 %copy.4 = f32[128,1024]{1,0:T(8,128)} copy(f32[128,1024]{1,0:T(8,128)} %get-tuple-element.6) | data formatting | bytes 1048576
